TPU v7x, 256 devices: a whole 4x4x8 slice. The times are simulated.
256 devices in a mesh: dp: 8 (over x, core), expert: 32 (over y, z).
Axes of the slice: x: 4, y: 4, z: 8, core: 2. Of those that a mesh axis runs over, the one named last changes fastest.
Arguments:
- tokens: bfloat16 [49152, 1024], P(('dp', 'expert')), may hold values from -6 to 6
- route_ids: int32 [49152, 4], P(('dp', 'expert')), may hold values from 0 to 31, all different within a row; in each aligned block of 192 rows (0 to 191, 192 to 383, ...) at most 36 rows name the same one
- gate_weight: float32 [49152, 4], P(('dp', 'expert')), may hold values from 0.25 to 1
- old_owner: int32 [32], replicated, may hold values from 0 to 31, as said below
- new_owner: int32 [32], replicated, may hold values from 0 to 31, as said below
- weights: bfloat16 [32, 3, 1024, 1024], P('expert', None, None, 'dp'), may hold values from -0.1875 to 0.1875
- first_moment: float32 [32, 3, 1024, 1024], P('expert', None, None, 'dp'), may hold values from -6 to 6
- second_moment: float32 [32, 3, 1024, 1024], P('expert', None, None, 'dp'), may hold values from 0.01 to 4
Outputs:
- layer_output: bfloat16 [49152, 1024], P(('dp', 'expert'))
- new_weights: bfloat16 [32, 3, 1024, 1024], P('expert', None, None, 'dp')
- new_first_moment: float32 [32, 3, 1024, 1024], P('expert', None, None, 'dp')
- new_second_moment: float32 [32, 3, 1024, 1024], P('expert', None, None, 'dp')
Inputs may be any that keep to these rules, and one draw needn't show every extreme that they name: `old_owner`: A permutation of the slots. `new_owner`: A permutation of the slots that differs from old_owner in exactly 5 experts. `route_ids`: the 4 experts of a row differ. In the 192 rows of one device no expert is named more than 36 times, a bound that some block reaches.
All inputs are finite; a program needn't handle non-finite values.
Results may differ from a plain program's by a relative error of at most 0.0058.
Values may be sent and summed in bfloat16 or wider, within the bound.
A program may use at most 128 MiB of HBM per device.

v0:
```python
import jax
import jax.numpy as jnp
from jax import lax
from jax.sharding import PartitionSpec as P


def relocate_weights(weights, source_slot):
    spread = lax.all_to_all(weights, "expert", split_axis=2, concat_axis=0, tiled=True)
    ordered = jnp.take(spread, source_slot, axis=0)
    return lax.all_to_all(ordered, "expert", split_axis=0, concat_axis=2, tiled=True)


def relocate_moments(first_moment, second_moment, source_slot):
    spread = (
        lax.all_to_all(first_moment, "expert", split_axis=2, concat_axis=0, tiled=True),
        lax.all_to_all(second_moment, "expert", split_axis=2, concat_axis=0, tiled=True),
    )
    ordered = (jnp.take(spread[0], source_slot, axis=0), jnp.take(spread[1], source_slot, axis=0))
    back = (
        lax.all_to_all(ordered[0], "expert", split_axis=0, concat_axis=2, tiled=True),
        lax.all_to_all(ordered[1], "expert", split_axis=0, concat_axis=2, tiled=True),
    )
    return (back[0], back[1])


def per_device(
    tokens, route_ids, gate_weight, old_owner, new_owner, weights, first_moment, second_moment
):
    peer_count = lax.axis_size("expert")
    tok_rows = tokens.shape[0]
    top_count = route_ids.shape[1]
    experts = old_owner.shape[0]
    capacity = max(2, 3 * tok_rows * top_count // (2 * experts))
    labels = jnp.arange(experts, dtype=jnp.int32)
    source_slot = jnp.sum(
        jnp.where(new_owner[None, :] == labels[:, None], old_owner[None, :], 0), axis=1
    )
    moved_first, moved_second = relocate_moments(first_moment, second_moment, source_slot)
    moved_weights = relocate_weights(weights, source_slot)
    expert_ids = route_ids.reshape(-1)
    target = jnp.sum(
        jnp.where(expert_ids[:, None] == labels[None, :], new_owner[None, :], 0), axis=1
    )
    matches = (target[:, None] == labels[None, :]).astype(jnp.int32)
    position = jnp.sum((jnp.cumsum(matches, axis=0) - 1) * matches, axis=1)
    slot_index = target * capacity + position
    slot_grid = slot_index.reshape(tok_rows, top_count)
    buffer_slots = jnp.arange(peer_count * capacity, dtype=jnp.int32)
    placement = jnp.any(slot_grid[None, :, :] == buffer_slots[:, None, None], axis=2).astype(
        jnp.bfloat16
    )
    outgoing = jnp.dot(placement, tokens, preferred_element_type=jnp.float32).astype(jnp.bfloat16)
    outgoing = outgoing.reshape(peer_count, capacity, tokens.shape[1])
    incoming = lax.all_to_all(outgoing, "expert", split_axis=0, concat_axis=0, tiled=True)
    received_rows = incoming.reshape(peer_count * capacity, tokens.shape[1])
    shard_piece = lax.all_gather(moved_weights, "dp", axis=3, tiled=True)
    gate_part = jnp.dot(received_rows, shard_piece[0, 0], preferred_element_type=jnp.float32)
    up_part = jnp.dot(received_rows, shard_piece[0, 1], preferred_element_type=jnp.float32)
    hidden = (jax.nn.silu(gate_part) * up_part).astype(jnp.bfloat16)
    accumulated = jnp.einsum(
        "rh,dh->rd", hidden, shard_piece[0, 2], preferred_element_type=jnp.float32
    )
    answers = accumulated.astype(jnp.bfloat16).reshape(peer_count, capacity, tokens.shape[1])
    returned = lax.all_to_all(answers, "expert", split_axis=0, concat_axis=0, tiled=True)
    returned = returned.reshape(peer_count * capacity, tokens.shape[1])
    picked = (
        jnp.take(returned, slot_index, axis=0)
        .astype(jnp.float32)
        .reshape(tok_rows, top_count, tokens.shape[1])
    )
    layer_output = jnp.sum(picked * gate_weight[:, :, None], axis=1).astype(jnp.bfloat16)
    return (layer_output, moved_weights, moved_first, moved_second)


def solution(mesh):
    placed = (
        P(("dp", "expert"), None),
        P(("dp", "expert"), None),
        P(("dp", "expert"), None),
        P(),
        P(),
        P("expert", None, None, "dp"),
        P("expert", None, None, "dp"),
        P("expert", None, None, "dp"),
    )
    return jax.shard_map(
        per_device,
        mesh=mesh,
        in_specs=placed,
        out_specs=(
            P(("dp", "expert"), None),
            P("expert", None, None, "dp"),
            P("expert", None, None, "dp"),
            P("expert", None, None, "dp"),
        ),
        check_vma=False,
    )
```

profile of v0, /device:TPU:2, one launch (start us, length us, event | category | flops | bytes accessed | tf_op | source)
XLA Modules:
  0.0 434.6 jit_solution(15613152316707516499)
XLA Ops:
  7.2 2.8 copy.43
  10.0 11.5 %all-to-all-start.1 = ((bf16[1,3,1024,128]{3,1,0,2:T(4,128)(2,1)}), bf16[1,3,1024,128]{3,1,0,2:T(4,128)(2,1)S(1)}, u32[]{:S(2)}, u32[]{:S(2)}) async-start(bf16[1,3,1024,128]{3,1,0,2:T(4,128)(2,1)} %copy.43), calls=%async_computation.1 | async-start | bytes 2097152 | tf_op jit(solution)/shard_map/all_to_all | solution.py:8
  21.7 28.5 %all-to-all-done.1 = bf16[1,3,1024,128]{3,1,0,2:T(4,128)(2,1)S(1)} async-done(((bf16[1,3,1024,128]{3,1,0,2:T(4,128)(2,1)}), bf16[1,3,1024,128]{3,1,0,2:T(4,128)(2,1)S(1)}, u32[]{:S(2)}, u32[]{:S(2)}) %all-to-all-start.1) | async-done | bytes 786464 | tf_op jit(solution)/shard_map/all_to_all | solution.py:8
  52.0 5.1 %all-to-all-start.2 = ((bf16[32,3,32,128]{3,2,1,0:T(8,128)(2,1)}), bf16[32,3,32,128]{3,2,1,0:T(8,128)(2,1)S(1)}, u32[]{:S(2)}, u32[]{:S(2)}) async-start(bf16[32,3,32,128]{3,2,1,0:T(8,128)(2,1)} %broadcast_select_fusion.2), calls=%async_computation.2 | async-start | bytes 1572864 | tf_op jit(solution)/shard_map/all_to_all | solution.py:10
  57.1 3.8 copy.48
  61.0 19.0 %all-to-all-done.2 = bf16[32,3,32,128]{3,2,1,0:T(8,128)(2,1)S(1)} async-done(((bf16[32,3,32,128]{3,2,1,0:T(8,128)(2,1)}), bf16[32,3,32,128]{3,2,1,0:T(8,128)(2,1)S(1)}, u32[]{:S(2)}, u32[]{:S(2)}) %all-to-all-start.2) | async-done | bytes 786464 | tf_op jit(solution)/shard_map/all_to_all | solution.py:10
  79.9 4.8 %all-to-all-start.4 = ((f32[1,3,1024,128]{3,1,0,2:T(4,128)}), f32[1,3,1024,128]{3,1,0,2:T(4,128)S(1)}, u32[]{:S(2)}, u32[]{:S(2)}) async-start(f32[1,3,1024,128]{3,1,0,2:T(4,128)} %copy.48), calls=%async_computation.4 | async-start | bytes 4194304 | tf_op jit(solution)/shard_map/all_to_all | solution.py:15
  84.7 3.9 copy.52
  88.6 45.7 %all-to-all-done.4 = f32[1,3,1024,128]{3,1,0,2:T(4,128)S(1)} async-done(((f32[1,3,1024,128]{3,1,0,2:T(4,128)}), f32[1,3,1024,128]{3,1,0,2:T(4,128)S(1)}, u32[]{:S(2)}, u32[]{:S(2)}) %all-to-all-start.4) | async-done | bytes 1572896 | tf_op jit(solution)/shard_map/all_to_all | solution.py:15
  134.3 6.0 %all-to-all-start.6 = ((f32[1,3,1024,128]{3,1,0,2:T(4,128)}), f32[1,3,1024,128]{3,1,0,2:T(4,128)}, u32[]{:S(2)}, u32[]{:S(2)}) async-start(f32[1,3,1024,128]{3,1,0,2:T(4,128)} %copy.52), calls=%async_computation.6 | async-start | bytes 4194304 | tf_op jit(solution)/shard_map/all_to_all | solution.py:16
  145.5 2.2 reshape.119
  147.7 42.2 %all-to-all-done.6 = f32[1,3,1024,128]{3,1,0,2:T(4,128)} async-done(((f32[1,3,1024,128]{3,1,0,2:T(4,128)}), f32[1,3,1024,128]{3,1,0,2:T(4,128)}, u32[]{:S(2)}, u32[]{:S(2)}) %all-to-all-start.6) | async-done | bytes 1572896 | tf_op jit(solution)/shard_map/all_to_all | solution.py:16
  189.9 6.0 %all-to-all-start = ((bf16[32,36,1024]{2,1,0:T(8,128)(2,1)}), bf16[32,36,1024]{2,1,0:T(8,128)(2,1)S(1)}, u32[]{:S(2)}, u32[]{:S(2)}) async-start(bf16[32,36,1024]{2,1,0:T(8,128)(2,1)} %reshape.119), calls=%async_computation | async-start | bytes 5242880 | tf_op jit(solution)/shard_map/all_to_all | solution.py:54
  195.9 2.9 copy.68
  198.9 2.9 copy.67
  201.8 3.2 gather_fusion.2
  205.1 3.2 gather_fusion.3
  208.2 4.1 broadcast_select_fusion
  212.4 46.4 %all-to-all-done = bf16[32,36,1024]{2,1,0:T(8,128)(2,1)S(1)} async-done(((bf16[32,36,1024]{2,1,0:T(8,128)(2,1)}), bf16[32,36,1024]{2,1,0:T(8,128)(2,1)S(1)}, u32[]{:S(2)}, u32[]{:S(2)}) %all-to-all-start) | async-done | bytes 2359328 | tf_op jit(solution)/shard_map/all_to_all | solution.py:54
  258.8 43.9 %all_to_all.118 = f32[32,3,32,128]{3,2,1,0:T(8,128)} all-to-all(f32[32,3,32,128]{3,2,1,0:T(8,128)} %get-tuple-element.6), channel_id=1, replica_groups=mesh['dp'=8,'expert'=32] {'expert'}, dimensions={0} | all-to-all | bytes 3145728 | tf_op jit(solution)/shard_map/all_to_all | solution.py:20
  302.7 5.2 %all-to-all-start.7 = ((f32[32,3,32,128]{3,2,1,0:T(8,128)}), f32[32,3,32,128]{3,2,1,0:T(8,128)}, u32[]{:S(2)}, u32[]{:S(2)}) async-start(f32[32,3,32,128]{3,2,1,0:T(8,128)} %get-tuple-element.5), calls=%async_computation.7 | async-start | bytes 3145728 | tf_op jit(solution)/shard_map/all_to_all | solution.py:21
  310.0 7.3 %fusion.2 = f32[1152,1024]{1,0:T(8,128)} fusion(bf16[1152,1024]{1,0:T(8,128)(2,1)} %reshape.120, bf16[1,3,1024,1024]{3,2,1,0:T(8,128)(2,1)} %all-gather.2.cloned.1.call-done), kind=kOutput, calls=%fused_computation.14 | convolution fusion | flops 2415919104 | bytes 9175040 | tf_op jit(solution)/shard_map/dot_general | solution.py:57
  317.3 10.2 %convolution_convert_fusion = bf16[1152,1024]{1,0:T(8,128)(2,1)} fusion(bf16[1,3,1024,1024]{3,2,1,0:T(8,128)(2,1)} %all-gather.2.cloned.1.call-done, bf16[1152,1024]{1,0:T(8,128)(2,1)S(1)} %copy-done.4, f32[1152,1024]{1,0:T(8,128)} %fusion.2), kind=kOutput, calls=%fused_computation.5 | convolution fusion | flops 4840095744 | bytes 13631488 | tf_op jit(solution)/shard_map/rh,dh->rd/dot_general | solution.py:60
  327.5 4.1 reshape.121
  331.6 15.0 %all-to-all-done.7 = f32[32,3,32,128]{3,2,1,0:T(8,128)} async-done(((f32[32,3,32,128]{3,2,1,0:T(8,128)}), f32[32,3,32,128]{3,2,1,0:T(8,128)}, u32[]{:S(2)}, u32[]{:S(2)}) %all-to-all-start.7) | async-done | bytes 1572896 | tf_op jit(solution)/shard_map/all_to_all | solution.py:21
  346.6 5.6 %all-to-all-start.3 = ((bf16[32,36,1024]{2,1,0:T(8,128)(2,1)}), bf16[32,36,1024]{2,1,0:T(8,128)(2,1)}, u32[]{:S(2)}, u32[]{:S(2)}) async-start(bf16[32,36,1024]{2,1,0:T(8,128)(2,1)} %reshape.121), calls=%async_computation.3 | async-start | bytes 5242880 | tf_op jit(solution)/shard_map/all_to_all | solution.py:64
  353.7 2.7 copy.55
  356.4 58.7 %all-to-all-done.3 = bf16[32,36,1024]{2,1,0:T(8,128)(2,1)} async-done(((bf16[32,36,1024]{2,1,0:T(8,128)(2,1)}), bf16[32,36,1024]{2,1,0:T(8,128)(2,1)}, u32[]{:S(2)}, u32[]{:S(2)}) %all-to-all-start.3) | async-done | bytes 2359328 | tf_op jit(solution)/shard_map/all_to_all | solution.py:64
  415.1 2.7 reshape.122
  417.7 3.6 gather_fusion.1
  421.3 2.5 gather.15
  423.8 3.9 multiply_reduce_fusion
  (50 shorter events, 10.8 us)
Async XLA Ops:
  7.2 137.5 %copy-start = (bf16[192,1024]{1,0:T(8,128)(2,1)S(1)}, bf16[192,1024]{1,0:T(8,128)(2,1)}, u32[]{:S(2)}) copy-start(bf16[192,1024]{1,0:T(8,128)(2,1)} %param.10) | copy-start | bytes 1179652
  7.2 14.3 %copy-start.7 = (s32[32]{0:T(128)S(1)}, s32[32]{0:T(128)}, u32[]{:S(2)}) copy-start(s32[32]{0:T(128)} %param.14) | copy-start | bytes 388
  7.2 14.3 %copy-start.8 = (s32[32]{0:T(128)S(1)}, s32[32]{0:T(128)}, u32[]{:S(2)}) copy-start(s32[32]{0:T(128)} %param.13) | copy-start | bytes 388
  10.0 40.1 %all-to-all-start.1 = ((bf16[1,3,1024,128]{3,1,0,2:T(4,128)(2,1)}), bf16[1,3,1024,128]{3,1,0,2:T(4,128)(2,1)S(1)}, u32[]{:S(2)}, u32[]{:S(2)}) async-start(bf16[1,3,1024,128]{3,1,0,2:T(4,128)(2,1)} %copy.43), calls=%async_computation.1 | async-start | bytes 2097152 | tf_op jit(solution)/shard_map/all_to_all | solution.py:8
  52.0 27.9 %all-to-all-start.2 = ((bf16[32,3,32,128]{3,2,1,0:T(8,128)(2,1)}), bf16[32,3,32,128]{3,2,1,0:T(8,128)(2,1)S(1)}, u32[]{:S(2)}, u32[]{:S(2)}) async-start(bf16[32,3,32,128]{3,2,1,0:T(8,128)(2,1)} %broadcast_select_fusion.2), calls=%async_computation.2 | async-start | bytes 1572864 | tf_op jit(solution)/shard_map/all_to_all | solution.py:10
  79.9 54.3 %all-to-all-start.4 = ((f32[1,3,1024,128]{3,1,0,2:T(4,128)}), f32[1,3,1024,128]{3,1,0,2:T(4,128)S(1)}, u32[]{:S(2)}, u32[]{:S(2)}) async-start(f32[1,3,1024,128]{3,1,0,2:T(4,128)} %copy.48), calls=%async_computation.4 | async-start | bytes 4194304 | tf_op jit(solution)/shard_map/all_to_all | solution.py:15
  88.6 52.7 %copy-start.5 = (s32[192,4]{0,1:T(4,128)S(1)}, s32[192,4]{0,1:T(4,128)}, u32[]{:S(2)}) copy-start(s32[192,4]{0,1:T(4,128)} %param.11) | copy-start | bytes 9220
  134.3 7.0 %copy-start.2 = (f32[1,3,1024,128]{3,1,0,2:T(4,128)}, f32[1,3,1024,128]{3,1,0,2:T(4,128)S(1)}, u32[]{:S(2)}) copy-start(f32[1,3,1024,128]{3,1,0,2:T(4,128)S(1)} %all-to-all-done.4) | copy-start | bytes 4718596
  134.3 55.6 %all-to-all-start.6 = ((f32[1,3,1024,128]{3,1,0,2:T(4,128)}), f32[1,3,1024,128]{3,1,0,2:T(4,128)}, u32[]{:S(2)}, u32[]{:S(2)}) async-start(f32[1,3,1024,128]{3,1,0,2:T(4,128)} %copy.52), calls=%async_computation.6 | async-start | bytes 4194304 | tf_op jit(solution)/shard_map/all_to_all | solution.py:16
  140.2 169.8 %all-gather.2.cloned.1.call-start = ((), (), s32[]{:S(2)}) async-start(), calls=%async_computation.8 | async-start | bytes 7077888 | tf_op jit(solution)/shard_map/all_gather | solution.py:56
  189.9 68.9 %all-to-all-start = ((bf16[32,36,1024]{2,1,0:T(8,128)(2,1)}), bf16[32,36,1024]{2,1,0:T(8,128)(2,1)S(1)}, u32[]{:S(2)}, u32[]{:S(2)}) async-start(bf16[32,36,1024]{2,1,0:T(8,128)(2,1)} %reshape.119), calls=%async_computation | async-start | bytes 5242880 | tf_op jit(solution)/shard_map/all_to_all | solution.py:54
  302.7 43.9 %all-to-all-start.7 = ((f32[32,3,32,128]{3,2,1,0:T(8,128)}), f32[32,3,32,128]{3,2,1,0:T(8,128)}, u32[]{:S(2)}, u32[]{:S(2)}) async-start(f32[32,3,32,128]{3,2,1,0:T(8,128)} %get-tuple-element.5), calls=%async_computation.7 | async-start | bytes 3145728 | tf_op jit(solution)/shard_map/all_to_all | solution.py:21
  310.0 7.3 %copy-start.4 = (bf16[1152,1024]{1,0:T(8,128)(2,1)S(1)}, bf16[1152,1024]{1,0:T(8,128)(2,1)}, u32[]{:S(2)}) copy-start(bf16[1152,1024]{1,0:T(8,128)(2,1)} %reshape.120) | copy-start | bytes 7077892
  331.6 20.6 %copy-start.6 = (f32[192,4]{0,1:T(4,128)S(1)}, f32[192,4]{0,1:T(4,128)}, u32[]{:S(2)}) copy-start(f32[192,4]{0,1:T(4,128)} %param.12) | copy-start | bytes 9220
  331.6 20.8 %copy-start.3 = (f32[32,3,32,128]{3,2,1,0:T(8,128)S(1)}, f32[32,3,32,128]{3,2,1,0:T(8,128)}, u32[]{:S(2)}) copy-start(f32[32,3,32,128]{3,2,1,0:T(8,128)} %all_to_all.118) | copy-start | bytes 4718596
  346.6 68.5 %all-to-all-start.3 = ((bf16[32,36,1024]{2,1,0:T(8,128)(2,1)}), bf16[32,36,1024]{2,1,0:T(8,128)(2,1)}, u32[]{:S(2)}, u32[]{:S(2)}) async-start(bf16[32,36,1024]{2,1,0:T(8,128)(2,1)} %reshape.121), calls=%async_computation.3 | async-start | bytes 5242880 | tf_op jit(solution)/shard_map/all_to_all | solution.py:64
  417.7 10.0 %copy-start.1 = (bf16[192,1024]{1,0:T(8,128)(2,1)S(1)}, bf16[192,1024]{1,0:T(8,128)(2,1)}, u32[]{:S(2)}) copy-start(bf16[192,1024]{1,0:T(8,128)(2,1)} %param.10) | copy-start | bytes 1179652
Sparse Core Ops, SparseCore 0:
  143.5 48.5 all-gather.1
where the time goes:
time: 436 us; the launch traced here: 435 us
  waiting for transfers between devices  255 us (58%)
  local copies, waits for them, and re-layouts  46.6 us (11%)
  starting transfers between devices  44.1 us (10%)
  blocking collectives  43.9 us (10%)
  matrix products  18.3 us (4%)
  between operations  14.3 us (3%)
  other arithmetic  11.9 us (3%)
    all_to_all x1, waiting for transfers between devices, per_device(): lax.all_to_all(answers, 'expert', split_axis=0, concat_axis=0, tiled=True)  58.7 us
    all_to_all x1, waiting for transfers between devices, per_device(): lax.all_to_all(outgoing, 'expert', split_axis=0, concat_axis=0, tiled=True)  46.4 us
    all_to_all x1, waiting for transfers between devices, relocate_moments(): lax.all_to_all(first_moment, 'expert', split_axis=2, concat_axis=0, tiled...  45.7 us
    all_to_all x1, blocking collectives, relocate_moments(): lax.all_to_all(ordered[0], 'expert', split_axis=0, concat_axis=2, tiled=T...  43.9 us
    all_to_all x1, waiting for transfers between devices, relocate_moments(): lax.all_to_all(second_moment, 'expert', split_axis=2, concat_axis=0, tile...  42.2 us
    all_to_all x1, waiting for transfers between devices, relocate_weights(): lax.all_to_all(weights, 'expert', split_axis=2, concat_axis=0, tiled=True)  28.5 us
    all_to_all x1, waiting for transfers between devices, relocate_weights(): lax.all_to_all(ordered, 'expert', split_axis=0, concat_axis=2, tiled=True)  19 us
    all_to_all x1, waiting for transfers between devices, relocate_moments(): lax.all_to_all(ordered[1], 'expert', split_axis=0, concat_axis=2, tiled=T...  15 us
  transfers between devices with their start and end apart: 8, of which 7 were waited for; matrix products, arithmetic and copies ran while one was open for 14% of the time, Pallas kernels for 0%

commit v1 on v0

--- a/solution.py
+++ b/solution.py
@@ -13,7 +13,12 @@
 def relocate_moments(first_moment, second_moment, source_slot):
     spread = (
         lax.all_to_all(first_moment, "expert", split_axis=2, concat_axis=0, tiled=True),
-        lax.all_to_all(second_moment, "expert", split_axis=2, concat_axis=0, tiled=True),
+        jnp.concatenate(
+            lax.all_to_all(
+                jnp.stack(jnp.split(second_moment, lax.axis_size("expert"), axis=2)), "expert", 0, 0
+            ),
+            axis=0,
+        ),
     )
     ordered = (jnp.take(spread[0], source_slot, axis=0), jnp.take(spread[1], source_slot, axis=0))
     back = (

time: 436 us -> 426 us (0.977)
  waiting for transfers between devices: 255 us -> 226 us
  local copies, waits for them, and re-layouts: 46.6 us -> 66.6 us
    unnamed x23 -> x55, local copies, waits for them, and re-layouts: 10.8 us -> 32.3 us
    all_to_all x1, waiting for transfers between devices: 28.5 us -> 12.9 us  [relocate_weights(): lax.all_to_all(weights, 'expert', split_axis=2, concat_axis=0, tiled=True)]
    all_to_all x1, waiting for transfers between devices: 42.2 us -> 34.8 us  [relocate_moments(): lax.all_to_all(jnp.stack(jnp.split(second_moment, lax.axis_size('expert')...]
    all_to_all x1, waiting for transfers between devices: 19 us -> 12.9 us  [relocate_weights(): lax.all_to_all(ordered, 'expert', split_axis=0, concat_axis=2, tiled=True)]
  transfers between devices with their start and end apart: 8 -> 8, of which waited for: 7 -> 7; matrix products, arithmetic and copies ran while one was open for 14% -> 18% of each run, Pallas kernels for 0% -> 0%
where the time goes in v1:
time: 426 us; the launch traced here: 425 us
  waiting for transfers between devices  226 us (53%)
  local copies, waits for them, and re-layouts  66.6 us (16%)
  blocking collectives  43.9 us (10%)
  starting transfers between devices  43.7 us (10%)
  matrix products  18.3 us (4%)
  between operations  14.4 us (3%)
  other arithmetic  11.9 us (3%)
    all_to_all x1, waiting for transfers between devices, per_device(): lax.all_to_all(answers, 'expert', split_axis=0, concat_axis=0, tiled=True)  58.7 us
    all_to_all x1, waiting for transfers between devices, per_device(): lax.all_to_all(outgoing, 'expert', split_axis=0, concat_axis=0, tiled=True)  49.4 us
    all_to_all x1, blocking collectives, relocate_moments(): lax.all_to_all(ordered[0], 'expert', split_axis=0, concat_axis=2, tiled=T...  43.9 us
    all_to_all x1, waiting for transfers between devices, relocate_moments(): lax.all_to_all(first_moment, 'expert', split_axis=2, concat_axis=0, tiled...  42.1 us
    all_to_all x1, waiting for transfers between devices, relocate_moments(): lax.all_to_all(jnp.stack(jnp.split(second_moment, lax.axis_size('expert')...  34.8 us
    unnamed x55, local copies, waits for them, and re-layouts  32.3 us
    all_to_all x1, waiting for transfers between devices, relocate_moments(): lax.all_to_all(ordered[1], 'expert', split_axis=0, concat_axis=2, tiled=T...  15 us
    all_to_all x1, waiting for transfers between devices, relocate_weights(): lax.all_to_all(weights, 'expert', split_axis=2, concat_axis=0, tiled=True)  12.9 us
  transfers between devices with their start and end apart: 8, of which 7 were waited for; matrix products, arithmetic and copies ran while one was open for 18% of the time, Pallas kernels for 0%

profile of v1, /device:TPU:2, one launch (start us, length us, event | category | flops | bytes accessed | tf_op | source)
XLA Modules:
  0.0 424.6 jit_solution(14267793212994621301)
XLA Ops:
  7.2 2.9 copy.41
  10.1 11.5 %all-to-all-start.1 = ((bf16[1,3,1024,128]{3,1,0,2:T(4,128)(2,1)}), bf16[1,3,1024,128]{3,1,0,2:T(4,128)(2,1)S(1)}, u32[]{:S(2)}, u32[]{:S(2)}) async-start(bf16[1,3,1024,128]{3,1,0,2:T(4,128)(2,1)} %copy.41), calls=%async_computation.1 | async-start | bytes 2097152 | tf_op jit(solution)/shard_map/all_to_all | solution.py:8
  37.4 12.9 %all-to-all-done.1 = bf16[1,3,1024,128]{3,1,0,2:T(4,128)(2,1)S(1)} async-done(((bf16[1,3,1024,128]{3,1,0,2:T(4,128)(2,1)}), bf16[1,3,1024,128]{3,1,0,2:T(4,128)(2,1)S(1)}, u32[]{:S(2)}, u32[]{:S(2)}) %all-to-all-start.1) | async-done | bytes 786464 | tf_op jit(solution)/shard_map/all_to_all | solution.py:8
  52.1 5.1 %all-to-all-start.2 = ((bf16[32,3,32,128]{3,2,1,0:T(8,128)(2,1)}), bf16[32,3,32,128]{3,2,1,0:T(8,128)(2,1)S(1)}, u32[]{:S(2)}, u32[]{:S(2)}) async-start(bf16[32,3,32,128]{3,2,1,0:T(8,128)(2,1)} %broadcast_select_fusion.2), calls=%async_computation.2 | async-start | bytes 1572864 | tf_op jit(solution)/shard_map/all_to_all | solution.py:10
  67.2 12.9 %all-to-all-done.2 = bf16[32,3,32,128]{3,2,1,0:T(8,128)(2,1)S(1)} async-done(((bf16[32,3,32,128]{3,2,1,0:T(8,128)(2,1)}), bf16[32,3,32,128]{3,2,1,0:T(8,128)(2,1)S(1)}, u32[]{:S(2)}, u32[]{:S(2)}) %all-to-all-start.2) | async-done | bytes 786464 | tf_op jit(solution)/shard_map/all_to_all | solution.py:10
  80.0 4.8 %all-to-all-start.6 = ((f32[32,1,3,32,128]{4,3,2,1,0:T(8,128)}), f32[32,1,3,32,128]{4,3,2,1,0:T(8,128)S(1)}, u32[]{:S(2)}, u32[]{:S(2)}) async-start(f32[32,1,3,32,128]{4,3,2,1,0:T(8,128)} %constant_dynamic-update-slice_fusion), calls=%async_computation.6 | async-start | bytes 3145728 | tf_op jit(solution)/shard_map/all_to_all | solution.py:17
  84.8 3.8 copy.46
  88.7 34.8 %all-to-all-done.6 = f32[32,1,3,32,128]{4,3,2,1,0:T(8,128)S(1)} async-done(((f32[32,1,3,32,128]{4,3,2,1,0:T(8,128)}), f32[32,1,3,32,128]{4,3,2,1,0:T(8,128)S(1)}, u32[]{:S(2)}, u32[]{:S(2)}) %all-to-all-start.6) | async-done | bytes 1572896 | tf_op jit(solution)/shard_map/all_to_all | solution.py:17
  124.6 5.6 %all-to-all-start.4 = ((f32[1,3,1024,128]{3,1,0,2:T(4,128)}), f32[1,3,1024,128]{3,1,0,2:T(4,128)}, u32[]{:S(2)}, u32[]{:S(2)}) async-start(f32[1,3,1024,128]{3,1,0,2:T(4,128)} %copy.46), calls=%async_computation.4 | async-start | bytes 4194304 | tf_op jit(solution)/shard_map/all_to_all | solution.py:15
  131.6 1.7 reduce-window.6
  135.5 2.3 reshape.122
  137.7 42.1 %all-to-all-done.4 = f32[1,3,1024,128]{3,1,0,2:T(4,128)} async-done(((f32[1,3,1024,128]{3,1,0,2:T(4,128)}), f32[1,3,1024,128]{3,1,0,2:T(4,128)}, u32[]{:S(2)}, u32[]{:S(2)}) %all-to-all-start.4) | async-done | bytes 1572896 | tf_op jit(solution)/shard_map/all_to_all | solution.py:15
  179.9 6.0 %all-to-all-start = ((bf16[32,36,1024]{2,1,0:T(8,128)(2,1)}), bf16[32,36,1024]{2,1,0:T(8,128)(2,1)S(1)}, u32[]{:S(2)}, u32[]{:S(2)}) async-start(bf16[32,36,1024]{2,1,0:T(8,128)(2,1)} %reshape.122), calls=%async_computation | async-start | bytes 5242880 | tf_op jit(solution)/shard_map/all_to_all | solution.py:59
  185.9 2.9 copy.59
  188.9 3.2 gather_fusion.3
  192.1 3.2 gather_fusion.2
  195.3 4.1 broadcast_select_fusion
  199.4 49.4 %all-to-all-done = bf16[32,36,1024]{2,1,0:T(8,128)(2,1)S(1)} async-done(((bf16[32,36,1024]{2,1,0:T(8,128)(2,1)}), bf16[32,36,1024]{2,1,0:T(8,128)(2,1)S(1)}, u32[]{:S(2)}, u32[]{:S(2)}) %all-to-all-start) | async-done | bytes 2359328 | tf_op jit(solution)/shard_map/all_to_all | solution.py:59
  248.8 43.9 %all_to_all.105 = f32[32,3,32,128]{3,2,1,0:T(8,128)} all-to-all(f32[32,3,32,128]{3,2,1,0:T(8,128)} %get-tuple-element.6), channel_id=1, replica_groups=mesh['dp'=8,'expert'=32] {'expert'}, dimensions={0} | all-to-all | bytes 3145728 | tf_op jit(solution)/shard_map/all_to_all | solution.py:25
  292.7 5.2 %all-to-all-start.7 = ((f32[32,3,32,128]{3,2,1,0:T(8,128)}), f32[32,3,32,128]{3,2,1,0:T(8,128)}, u32[]{:S(2)}, u32[]{:S(2)}) async-start(f32[32,3,32,128]{3,2,1,0:T(8,128)} %get-tuple-element.5), calls=%async_computation.7 | async-start | bytes 3145728 | tf_op jit(solution)/shard_map/all_to_all | solution.py:26
  297.9 2.1 reshape.123
  300.0 7.3 %fusion.2 = f32[1152,1024]{1,0:T(8,128)} fusion(bf16[1152,1024]{1,0:T(8,128)(2,1)} %reshape.123, bf16[1,3,1024,1024]{3,2,1,0:T(8,128)(2,1)} %all-gather.2.cloned.1.call-done), kind=kOutput, calls=%fused_computation.14 | convolution fusion | flops 2415919104 | bytes 9175040 | tf_op jit(solution)/shard_map/dot_general | solution.py:62
  307.3 10.2 %convolution_convert_fusion = bf16[1152,1024]{1,0:T(8,128)(2,1)} fusion(bf16[1,3,1024,1024]{3,2,1,0:T(8,128)(2,1)} %all-gather.2.cloned.1.call-done, bf16[1152,1024]{1,0:T(8,128)(2,1)S(1)} %copy-done.4, f32[1152,1024]{1,0:T(8,128)} %fusion.2), kind=kOutput, calls=%fused_computation.5 | convolution fusion | flops 4840095744 | bytes 13631488 | tf_op jit(solution)/shard_map/rh,dh->rd/dot_general | solution.py:65
  317.5 4.1 reshape.124
  321.5 15.0 %all-to-all-done.7 = f32[32,3,32,128]{3,2,1,0:T(8,128)} async-done(((f32[32,3,32,128]{3,2,1,0:T(8,128)}), f32[32,3,32,128]{3,2,1,0:T(8,128)}, u32[]{:S(2)}, u32[]{:S(2)}) %all-to-all-start.7) | async-done | bytes 1572896 | tf_op jit(solution)/shard_map/all_to_all | solution.py:26
  336.6 5.6 %all-to-all-start.3 = ((bf16[32,36,1024]{2,1,0:T(8,128)(2,1)}), bf16[32,36,1024]{2,1,0:T(8,128)(2,1)}, u32[]{:S(2)}, u32[]{:S(2)}) async-start(bf16[32,36,1024]{2,1,0:T(8,128)(2,1)} %reshape.124), calls=%async_computation.3 | async-start | bytes 5242880 | tf_op jit(solution)/shard_map/all_to_all | solution.py:69
  343.7 2.7 copy.50
  346.4 58.7 %all-to-all-done.3 = bf16[32,36,1024]{2,1,0:T(8,128)(2,1)} async-done(((bf16[32,36,1024]{2,1,0:T(8,128)(2,1)}), bf16[32,36,1024]{2,1,0:T(8,128)(2,1)}, u32[]{:S(2)}, u32[]{:S(2)}) %all-to-all-start.3) | async-done | bytes 2359328 | tf_op jit(solution)/shard_map/all_to_all | solution.py:69
  405.1 2.7 reshape.125
  407.7 3.6 gather_fusion.1
  411.3 2.5 gather.15
  413.8 3.9 multiply_reduce_fusion
  (82 shorter events, 33.6 us)
Async XLA Ops:
  7.2 127.5 %copy-start = (bf16[192,1024]{1,0:T(8,128)(2,1)S(1)}, bf16[192,1024]{1,0:T(8,128)(2,1)}, u32[]{:S(2)}) copy-start(bf16[192,1024]{1,0:T(8,128)(2,1)} %param.10) | copy-start | bytes 1179652
  7.2 14.4 %copy-start.8 = (s32[32]{0:T(128)S(1)}, s32[32]{0:T(128)}, u32[]{:S(2)}) copy-start(s32[32]{0:T(128)} %param.14) | copy-start | bytes 388
  7.2 14.4 %copy-start.9 = (s32[32]{0:T(128)S(1)}, s32[32]{0:T(128)}, u32[]{:S(2)}) copy-start(s32[32]{0:T(128)} %param.13) | copy-start | bytes 388
  7.2 14.6 %copy-start.5 = (f32[1,3,1024,128]{3,2,1,0:T(8,128)S(1)}, f32[1,3,1024,128]{3,2,1,0:T(8,128)}, u32[]{:S(2)}) copy-start(f32[1,3,1024,128]{3,2,1,0:T(8,128)} %param.17) | copy-start | bytes 4718596
  10.1 40.1 %all-to-all-start.1 = ((bf16[1,3,1024,128]{3,1,0,2:T(4,128)(2,1)}), bf16[1,3,1024,128]{3,1,0,2:T(4,128)(2,1)S(1)}, u32[]{:S(2)}, u32[]{:S(2)}) async-start(bf16[1,3,1024,128]{3,1,0,2:T(4,128)(2,1)} %copy.41), calls=%async_computation.1 | async-start | bytes 2097152 | tf_op jit(solution)/shard_map/all_to_all | solution.py:8
  52.1 27.9 %all-to-all-start.2 = ((bf16[32,3,32,128]{3,2,1,0:T(8,128)(2,1)}), bf16[32,3,32,128]{3,2,1,0:T(8,128)(2,1)S(1)}, u32[]{:S(2)}, u32[]{:S(2)}) async-start(bf16[32,3,32,128]{3,2,1,0:T(8,128)(2,1)} %broadcast_select_fusion.2), calls=%async_computation.2 | async-start | bytes 1572864 | tf_op jit(solution)/shard_map/all_to_all | solution.py:10
  80.0 43.4 %all-to-all-start.6 = ((f32[32,1,3,32,128]{4,3,2,1,0:T(8,128)}), f32[32,1,3,32,128]{4,3,2,1,0:T(8,128)S(1)}, u32[]{:S(2)}, u32[]{:S(2)}) async-start(f32[32,1,3,32,128]{4,3,2,1,0:T(8,128)} %constant_dynamic-update-slice_fusion), calls=%async_computation.6 | async-start | bytes 3145728 | tf_op jit(solution)/shard_map/all_to_all | solution.py:17
  123.5 1.1 copy-start.3
  124.6 55.3 %all-to-all-start.4 = ((f32[1,3,1024,128]{3,1,0,2:T(4,128)}), f32[1,3,1024,128]{3,1,0,2:T(4,128)}, u32[]{:S(2)}, u32[]{:S(2)}) async-start(f32[1,3,1024,128]{3,1,0,2:T(4,128)} %copy.46), calls=%async_computation.4 | async-start | bytes 4194304 | tf_op jit(solution)/shard_map/all_to_all | solution.py:15
  130.2 1.0 copy-start.6
  130.3 169.7 %all-gather.2.cloned.1.call-start = ((), (), s32[]{:S(2)}) async-start(), calls=%async_computation.8 | async-start | bytes 7077888 | tf_op jit(solution)/shard_map/all_gather | solution.py:61
  179.9 68.9 %all-to-all-start = ((bf16[32,36,1024]{2,1,0:T(8,128)(2,1)}), bf16[32,36,1024]{2,1,0:T(8,128)(2,1)S(1)}, u32[]{:S(2)}, u32[]{:S(2)}) async-start(bf16[32,36,1024]{2,1,0:T(8,128)(2,1)} %reshape.122), calls=%async_computation | async-start | bytes 5242880 | tf_op jit(solution)/shard_map/all_to_all | solution.py:59
  292.7 43.9 %all-to-all-start.7 = ((f32[32,3,32,128]{3,2,1,0:T(8,128)}), f32[32,3,32,128]{3,2,1,0:T(8,128)}, u32[]{:S(2)}, u32[]{:S(2)}) async-start(f32[32,3,32,128]{3,2,1,0:T(8,128)} %get-tuple-element.5), calls=%async_computation.7 | async-start | bytes 3145728 | tf_op jit(solution)/shard_map/all_to_all | solution.py:26
  300.0 7.3 %copy-start.4 = (bf16[1152,1024]{1,0:T(8,128)(2,1)S(1)}, bf16[1152,1024]{1,0:T(8,128)(2,1)}, u32[]{:S(2)}) copy-start(bf16[1152,1024]{1,0:T(8,128)(2,1)} %reshape.123) | copy-start | bytes 7077892
  321.5 20.6 %copy-start.7 = (f32[192,4]{0,1:T(4,128)S(1)}, f32[192,4]{0,1:T(4,128)}, u32[]{:S(2)}) copy-start(f32[192,4]{0,1:T(4,128)} %param.12) | copy-start | bytes 9220
  321.5 20.9 %copy-start.2 = (f32[32,3,32,128]{3,2,1,0:T(8,128)S(1)}, f32[32,3,32,128]{3,2,1,0:T(8,128)}, u32[]{:S(2)}) copy-start(f32[32,3,32,128]{3,2,1,0:T(8,128)} %all_to_all.105) | copy-start | bytes 4718596
  336.6 68.5 %all-to-all-start.3 = ((bf16[32,36,1024]{2,1,0:T(8,128)(2,1)}), bf16[32,36,1024]{2,1,0:T(8,128)(2,1)}, u32[]{:S(2)}, u32[]{:S(2)}) async-start(bf16[32,36,1024]{2,1,0:T(8,128)(2,1)} %reshape.124), calls=%async_computation.3 | async-start | bytes 5242880 | tf_op jit(solution)/shard_map/all_to_all | solution.py:69
  411.3 6.5 %copy-start.1 = (bf16[192,1024]{1,0:T(8,128)(2,1)S(1)}, bf16[192,1024]{1,0:T(8,128)(2,1)}, u32[]{:S(2)}) copy-start(bf16[192,1024]{1,0:T(8,128)(2,1)} %param.10) | copy-start | bytes 1179652
Sparse Core Ops, SparseCore 0:
  133.5 48.5 all-gather.1
